TPU v7x, 32 devices: a whole 2x2x4 slice. The times are simulated.
32 devices in a mesh: section: 4 (over y, x), dp: 2 (over core), mp: 4 (over z).
Axes of the slice: x: 2, y: 2, z: 4, core: 2. Of those that a mesh axis runs over, the one named last changes fastest.
Arguments:
- enc_hidden: bfloat16 [2, 128, 4096], P('dp', None, ('section', 'mp')), may hold values from -32 to 32
- enc_gain: float32 [4096], replicated, may hold values from 0.1 to 1.9
- key_weight: bfloat16 [4, 4096, 2048], P('section', None, 'mp'), may hold values from -0.09375 to 0.09375
- value_weight: bfloat16 [4, 4096, 2048], P('section', None, 'mp'), may hold values from -0.25 to 0.25
- queries: bfloat16 [2, 4, 256, 2048], P('dp', 'section', None, 'mp'), may hold values from -256 to 256
- out_grad: bfloat16 [2, 4, 256, 2048], P('dp', 'section', None, 'mp'), may hold values from -4 to 4
Outputs:
- attended: bfloat16 [2, 4, 256, 2048], P('dp', 'section', None, 'mp')
- query_grad: bfloat16 [2, 4, 256, 2048], P('dp', 'section', None, 'mp')
- hidden_grad: float32 [2, 128, 4096], P('dp', None, ('section', 'mp'))
- gain_grad: float32 [4096], P(('section', 'mp'))
All inputs are finite; a program needn't handle non-finite values.
Results may differ from a plain program's by a relative error of at most 0.02.
The roundings to bfloat16 on the way count: a program that leaves them out, or rounds other values in their place, can miss the bound.
Values may be sent and summed in bfloat16 or wider, within the bound.
No kernel may reach another device: no remote copies, remote signals or barrier semaphores. Data moves between devices by JAX's collectives and lax.ppermute only.
A program may use at most 64 MiB of HBM per device.

v0:
```python
import jax
import jax.numpy as jnp
from jax import lax
from jax.sharding import PartitionSpec as P

DH = 64
epsilon = 1e-06


def attend(key_value, queries, out_grad, columns):
    batch, source_length, _ = key_value.shape
    head_count = columns // DH
    factor = DH ** (-0.5)
    keys = key_value[..., :columns].reshape(batch, source_length, head_count, DH)
    values = key_value[..., columns:].reshape(batch, source_length, head_count, DH)
    asked = queries[:, 0].reshape(batch, -1, head_count, DH)
    upstream = out_grad[:, 0].reshape(batch, -1, head_count, DH)
    target_length = asked.shape[1]
    scores = jnp.einsum("sqhd,skhd->shqk", asked, keys, preferred_element_type=jnp.float32) * factor
    highest = jnp.max(scores, axis=-1, keepdims=True)
    raised = jnp.exp(scores - highest)
    shares = raised / jnp.sum(raised, axis=-1, keepdims=True)
    shares_low = shares.astype(jnp.bfloat16)
    attended = jnp.einsum(
        "shqk,skhd->sqhd", shares_low, values, preferred_element_type=jnp.float32
    ).astype(jnp.bfloat16)
    share_grad = jnp.einsum("sqhd,skhd->shqk", upstream, values, preferred_element_type=jnp.float32)
    value_grad = jnp.einsum(
        "shqk,sqhd->skhd", shares_low, upstream, preferred_element_type=jnp.float32
    ).astype(jnp.bfloat16)
    score_grad = (
        shares * (share_grad - jnp.sum(shares * share_grad, axis=-1, keepdims=True)) * factor
    )
    score_low = score_grad.astype(jnp.bfloat16)
    query_grad = jnp.einsum(
        "shqk,skhd->sqhd", score_low, keys, preferred_element_type=jnp.float32
    ).astype(jnp.bfloat16)
    key_grad = jnp.einsum(
        "shqk,sqhd->skhd", score_low, asked, preferred_element_type=jnp.float32
    ).astype(jnp.bfloat16)
    return (
        attended.reshape(batch, 1, target_length, columns),
        query_grad.reshape(batch, 1, target_length, columns),
        key_grad.reshape(batch, source_length, columns),
        value_grad.reshape(batch, source_length, columns),
    )


def per_device(enc_hidden, enc_gain, key_weight, value_weight, queries, out_grad):
    batch, source_length, own_columns = enc_hidden.shape
    width = key_weight.shape[1]
    columns = key_weight.shape[2]
    key_matrix = key_weight[0]
    value_matrix = value_weight[0]
    replicas = batch * lax.axis_size("dp")
    sections = lax.axis_size("section")
    groups = lax.axis_size("mp")
    first_column = lax.axis_index(("section", "mp")) * own_columns
    gain_own = lax.dynamic_slice_in_dim(enc_gain, first_column, own_columns, 0)
    widened = enc_hidden.astype(jnp.float32)
    squares = lax.psum(jnp.sum(widened * widened, axis=-1, keepdims=True), ("section", "mp"))
    inverse = lax.rsqrt(squares / width + epsilon)
    normed = widened * inverse
    own_memory = (normed * gain_own).astype(jnp.bfloat16)
    memory = lax.all_gather(own_memory, ("section", "mp"), axis=2, tiled=True)
    flat = memory.reshape(-1, width)
    keys = jnp.dot(flat, key_matrix, preferred_element_type=jnp.float32).astype(jnp.bfloat16)
    values = jnp.dot(flat, value_matrix, preferred_element_type=jnp.float32).astype(jnp.bfloat16)
    key_value = jnp.concatenate((keys, values), axis=-1).reshape(batch, source_length, 2 * columns)
    attended, query_grad, key_grad, value_grad = attend(key_value, queries, out_grad, columns)
    total = jnp.einsum("skc,dc->skd", key_grad, key_matrix, preferred_element_type=jnp.float32)
    head_part = (
        total
        + jnp.einsum("skc,dc->skd", value_grad, value_matrix, preferred_element_type=jnp.float32)
    ).reshape(batch, source_length, sections, groups, own_columns)
    layer_part = lax.psum_scatter(
        head_part.astype(jnp.bfloat16), "mp", scatter_dimension=3, tiled=True
    )
    own_grad = (
        lax.psum_scatter(layer_part, "section", scatter_dimension=2, tiled=True)
        .astype(jnp.float32)
        .reshape(batch, source_length, own_columns)
    )
    scaled = own_grad * gain_own
    mean_total = lax.psum(jnp.sum(scaled * normed, axis=-1, keepdims=True), ("section", "mp"))
    gain_total = lax.psum(jnp.sum(own_grad * normed, axis=(0, 1)), "dp")
    hidden_grad = inverse * (scaled - normed * (mean_total / width))
    gain_grad = gain_total / replicas
    return (attended, query_grad, hidden_grad, gain_grad)


def solution(mesh):
    in_specs = (
        P("dp", None, ("section", "mp")),
        P(),
        P("section", None, "mp"),
        P("section", None, "mp"),
        P("dp", "section", None, "mp"),
        P("dp", "section", None, "mp"),
    )
    out_specs = (
        P("dp", "section", None, "mp"),
        P("dp", "section", None, "mp"),
        P("dp", None, ("section", "mp")),
        P(("section", "mp")),
    )
    return jax.shard_map(
        per_device, mesh=mesh, in_specs=in_specs, out_specs=out_specs, check_vma=False
    )
```

profile of v0, /device:TPU:0, one launch (start us, length us, event | category | flops | bytes accessed | tf_op | source)
XLA Modules:
  0.0 253.4 jit_solution(6738457621057778831)
XLA Ops:
  7.2 0.0 all-gather.2.cloned.1.call-start
  7.2 0.9 fusion.40
  8.2 43.7 %psum.21 = f32[1,128,1]{1,2,0:T(1,128)S(1)} all-reduce(f32[1,128,1]{1,2,0:T(1,128)S(1)} %bitcast.127), channel_id=1, replica_groups=mesh['section'=4,'dp'=2,'mp'=4] {'section','mp'}, use_global_device_ids=true, to_apply=%region_1.0 | all-reduce | flops 128 | bytes 1024 | tf_op jit(solution)/shard_map/psum | solution.py:61
  51.9 0.8 dynamic_slice.3
  52.7 1.6 fusion.38
  54.2 0.0 all-gather.2.cloned.1.call-update
  54.2 0.0 all-reduce.4.cloned.1.call-start
  54.3 1.1 copy.38
  55.4 1.1 copy.40
  56.5 49.2 %all-gather.2.cloned.1.call-done = bf16[1,128,4096]{2,1,0:T(8,128)(2,1)} async-done(((bf16[1,128,256]{2,1,0:T(8,128)(2,1)}), bf16[1,128,4096]{2,1,0:T(8,128)(2,1)}) %all-gather.2.cloned.1.call-update) | async-done | bytes 1048592 | tf_op jit(solution)/shard_map/all_gather | solution.py:65
  105.7 0.0 copy-start.1
  105.7 0.0 copy-start.2
  105.7 3.4 %fusion.20 = bf16[128,512]{1,0:T(8,128)(2,1)S(1)} fusion(bf16[1,4096,512]{2,1,0:T(8,128)(2,1)} %param.9, bf16[1,128,4096]{2,1,0:T(8,128)(2,1)} %all-gather.2.cloned.1.call-done), kind=kOutput, calls=%fused_computation.23 | convolution fusion | flops 536936448 | bytes 5373952 | tf_op jit(solution)/shard_map/dot_general | solution.py:68
  109.1 0.4 copy-done.1
  109.4 0.3 copy-done.2
  109.7 0.8 fusion.17
  110.6 0.1 copy.36
  110.7 0.1 copy.37
  110.8 0.0 copy-start.4
  110.8 1.5 fusion.49
  112.3 0.0 copy-start.7
  112.3 0.3 convolution_bitcast_fusion
  112.7 0.7 convolution_convert_fusion.2
  113.4 2.0 convolution_convert_fusion.3
  115.4 0.0 copy-done.4
  115.4 0.0 copy-done.7
  115.4 0.0 copy-start
  115.4 3.8 %fusion.6 = f32[128,4096]{1,0:T(8,128)S(1)} fusion(bf16[128,512]{0,1:T(8,128)(2,1)S(1)} %bitcast.121, bf16[1,4096,512]{2,1,0:T(8,128)(2,1)} %param.8), kind=kOutput, calls=%fused_computation.7 | convolution fusion | flops 536870912 | bytes 6422528 | tf_op jit(solution)/shard_map/skc,dc->skd/dot_general | solution.py:71
  119.2 0.0 copy-done
  119.3 1.5 fusion.2
  120.8 0.0 copy-start.6
  120.8 0.8 convert_element_type.98
  121.6 0.0 copy-start.5
  121.6 0.0 copy-start.8
  121.6 1.3 copy.44
  122.9 0.0 all-reduce.4.cloned.1.call-update
  122.9 0.0 reduce-scatter.10.cloned.1.call-start
  123.0 0.0 copy-done.6
  123.0 0.6 dynamic-slice
  123.6 50.1 %all-reduce.4.cloned.1.call-done = bf16[1,128,4,4,256]{4,1,3,2,0:T(8,128)(2,1)} async-done(((bf16[1,128,4,4,256]{4,1,3,2,0:T(8,128)(2,1)}), bf16[1,128,4,4,256]{4,1,3,2,0:T(8,128)(2,1)}) %all-reduce.4.cloned.1.call-update) | async-done | bytes 1048592
  173.7 2.3 constant_dynamic-slice_fusion
  176.1 0.0 reduce-scatter.10.cloned.1.call-update
  176.1 1.6 convolution_convert_fusion.1
  177.7 0.0 copy-start.3
  177.7 0.8 copy.45
  178.5 0.0 copy-done.5
  178.6 0.0 copy-done.8
  178.6 2.0 convolution_convert_fusion
  180.6 0.8 copy.46
  181.4 18.8 %reduce-scatter.10.cloned.1.call-done = bf16[1,128,1,1,256]{4,1,3,2,0:T(8,128)(2,1)} async-done(((bf16[1,128,4,1,256]{4,1,3,2,0:T(8,128)(2,1)}), bf16[1,128,1,1,256]{4,1,3,2,0:T(8,128)(2,1)}) %reduce-scatter.10.cloned.1.call-update) | async-done | bytes 65552
  200.2 0.0 copy-done.3
  200.2 1.0 fusion.41
  201.3 41.0 %psum.22 = f32[1,128,1]{1,2,0:T(1,128)S(1)} all-reduce(f32[1,128,1]{1,2,0:T(1,128)S(1)} %bitcast.126), channel_id=1, replica_groups=mesh['section'=4,'dp'=2,'mp'=4] {'section','mp'}, use_global_device_ids=true, to_apply=%region_8.0 | all-reduce | flops 128 | bytes 1024 | tf_op jit(solution)/shard_map/psum | solution.py:85
  242.2 2.5 psum.23
  244.7 0.6 broadcast_multiply_fusion
  245.3 1.6 fusion.37
  (4 shorter events, 0.1 us)
Async XLA Ops:
  7.2 98.5 %all-gather.2.cloned.1.call-start = ((), (), s32[]{:S(2)}) async-start(), calls=%async_computation.1 | async-start | bytes 1114112 | tf_op jit(solution)/shard_map/all_gather | solution.py:65
  54.2 119.5 %all-reduce.4.cloned.1.call-start = ((), (), s32[]{:S(2)}) async-start(), calls=%async_computation.2 | async-start | bytes 2097152
  105.7 3.7 %copy-start.1 = (bf16[1,4096,512]{2,1,0:T(8,128)(2,1)S(1)}, bf16[1,4096,512]{2,1,0:T(8,128)(2,1)}, u32[]{:S(2)}) copy-start(bf16[1,4096,512]{2,1,0:T(8,128)(2,1)} %param.8) | copy-start | bytes 12582916
  105.7 4.0 %copy-start.2 = (bf16[1,128,4096]{2,1,0:T(8,128)(2,1)S(1)}, bf16[1,128,4096]{2,1,0:T(8,128)(2,1)}, u32[]{:S(2)}) copy-start(bf16[1,128,4096]{2,1,0:T(8,128)(2,1)} %all-gather.2.cloned.1.call-done) | copy-start | bytes 3145732
  110.8 4.5 %copy-start.4 = (bf16[1,128,512]{1,2,0:T(8,128)(2,1)}, bf16[1,128,512]{1,2,0:T(8,128)(2,1)S(1)}, u32[]{:S(2)}) copy-start(bf16[1,128,512]{1,2,0:T(8,128)(2,1)S(1)} %copy.37) | copy-start | bytes 393220
  112.3 3.1 %copy-start.7 = (f32[8,256]{1,0:T(8,128)}, f32[8,256]{1,0:T(8,128)S(1)}, u32[]{:S(2)}) copy-start(f32[8,256]{1,0:T(8,128)S(1)} %get-tuple-element.20) | copy-start | bytes 24580
  115.4 3.8 %copy-start = (bf16[1,4096,512]{2,1,0:T(8,128)(2,1)S(1)}, bf16[1,4096,512]{2,1,0:T(8,128)(2,1)}, u32[]{:S(2)}) copy-start(bf16[1,4096,512]{2,1,0:T(8,128)(2,1)} %param.9) | copy-start | bytes 12582916
  120.8 2.3 copy-start.6
  121.6 57.0 %copy-start.5 = (bf16[1,128,512]{1,2,0:T(8,128)(2,1)S(1)}, bf16[1,128,512]{1,2,0:T(8,128)(2,1)}, u32[]{:S(2)}) copy-start(bf16[1,128,512]{1,2,0:T(8,128)(2,1)} %copy-done.4) | copy-start | bytes 393220
  121.6 57.0 %copy-start.8 = (f32[8,256]{1,0:T(8,128)S(1)}, f32[8,256]{1,0:T(8,128)}, u32[]{:S(2)}) copy-start(f32[8,256]{1,0:T(8,128)} %copy-done.7) | copy-start | bytes 24580
  122.9 77.3 %reduce-scatter.10.cloned.1.call-start = ((), (), s32[]{:S(2)}) async-start(), calls=%async_computation.3 | async-start | bytes 327680
  177.7 22.5 %copy-start.3 = (bf16[1,128,256]{2,1,0:T(8,128)(2,1)S(1)}, bf16[1,128,256]{2,1,0:T(8,128)(2,1)}, u32[]{:S(2)}) copy-start(bf16[1,128,256]{2,1,0:T(8,128)(2,1)} %param.6) | copy-start | bytes 196612
Sparse Core Ops, SparseCore 0:
  54.4 51.2 all-gather.1
  123.1 50.6 all-reduce.3
  176.7 23.4 reduce-scatter.9
where the time goes:
time: 254 us; the launch traced here: 253 us
  waiting for transfers between devices  118 us (46%)
  blocking collectives  87.1 us (34%)
  matrix products  17.6 us (7%)
  between operations  14 us (6%)
  local copies, waits for them, and re-layouts  10.6 us (4%)
  other arithmetic  5.72 us (2%)
    unnamed x5, waiting for transfers between devices  69 us
    all_gather x1, waiting for transfers between devices, per_device(): memory = lax.all_gather(own_memory, ('section', 'mp'), axis=2, tiled=True)  49.2 us
    psum x1, blocking collectives, per_device(): lax.psum(jnp.sum(widened * widened, axis=-1, keepdims=True), ('section',...  43.7 us
    psum x1, blocking collectives, per_device(): lax.psum(jnp.sum(scaled * normed, axis=-1, keepdims=True), ('section', 'm...  41 us
    unnamed x24, local copies, waits for them, and re-layouts  7.49 us
  transfers between devices with their start and end apart: 3, of which 3 were waited for; matrix products, arithmetic and copies ran while one was open for 3% of the time, Pallas kernels for 0%

commit v1 on v0

--- a/solution.py
+++ b/solution.py
@@ -58,7 +58,9 @@
     first_column = lax.axis_index(("section", "mp")) * own_columns
     gain_own = lax.dynamic_slice_in_dim(enc_gain, first_column, own_columns, 0)
     widened = enc_hidden.astype(jnp.float32)
-    squares = lax.psum(jnp.sum(widened * widened, axis=-1, keepdims=True), ("section", "mp"))
+    squares = jnp.sum(widened * widened, axis=-1, keepdims=True)
+    for name in ("mp", "section"):
+        squares = lax.psum(squares, name)
     inverse = lax.rsqrt(squares / width + epsilon)
     normed = widened * inverse
     own_memory = (normed * gain_own).astype(jnp.bfloat16)

time: 254 us -> 234 us (0.921)
  blocking collectives: 87.1 us -> 66.8 us
    psum x1 -> x2, blocking collectives: 43.7 us -> 23.4 us  [per_device(): squares = lax.psum(squares, name)]
where the time goes in v1:
time: 234 us; the launch traced here: 233 us
  waiting for transfers between devices  118 us (50%)
  blocking collectives  66.8 us (29%)
  matrix products  17.6 us (8%)
  between operations  13.9 us (6%)
  local copies, waits for them, and re-layouts  10.6 us (5%)
  other arithmetic  5.72 us (2%)
    unnamed x5, waiting for transfers between devices  69 us
    all_gather x1, waiting for transfers between devices, per_device(): memory = lax.all_gather(own_memory, ('section', 'mp'), axis=2, tiled=True)  49.3 us
    psum x1, blocking collectives, per_device(): lax.psum(jnp.sum(scaled * normed, axis=-1, keepdims=True), ('section', 'm...  41 us
    psum x2, blocking collectives, per_device(): squares = lax.psum(squares, name)  23.4 us
    unnamed x24, local copies, waits for them, and re-layouts  7.49 us
  transfers between devices with their start and end apart: 3, of which 3 were waited for; matrix products, arithmetic and copies ran while one was open for 3% of the time, Pallas kernels for 0%

profile of v1, /device:TPU:0, one launch (start us, length us, event | category | flops | bytes accessed | tf_op | source)
XLA Modules:
  0.0 233.2 jit_solution(10809075548189412303)
XLA Ops:
  7.2 0.0 all-gather.2.cloned.1.call-start
  7.2 0.9 fusion.40
  8.2 13.5 %psum.28 = f32[1,128,1]{1,2,0:T(1,128)S(1)} all-reduce(f32[1,128,1]{1,2,0:T(1,128)S(1)} %bitcast.127), channel_id=1, replica_groups=mesh['section'=4,'dp'=2,'mp'=4] {'mp'}, use_global_device_ids=true, to_apply=%region_1.0 | all-reduce | flops 128 | bytes 1024 | tf_op jit(solution)/shard_map/psum | solution.py:63
  21.6 9.9 %psum.29 = f32[1,128,1]{1,2,0:T(1,128)S(1)} all-reduce(f32[1,128,1]{1,2,0:T(1,128)S(1)} %psum.28), channel_id=1, replica_groups=mesh['section'=4,'dp'=2,'mp'=4] {'section'}, use_global_device_ids=true, to_apply=%region_2.0 | all-reduce | flops 128 | bytes 1024 | tf_op jit(solution)/shard_map/psum | solution.py:63
  31.5 0.8 dynamic_slice.3
  32.3 1.6 fusion.38
  33.8 0.0 all-gather.2.cloned.1.call-update
  33.9 0.0 all-reduce.4.cloned.1.call-start
  33.9 1.1 copy.38
  35.0 1.1 copy.40
  36.1 49.3 %all-gather.2.cloned.1.call-done = bf16[1,128,4096]{2,1,0:T(8,128)(2,1)} async-done(((bf16[1,128,256]{2,1,0:T(8,128)(2,1)}), bf16[1,128,4096]{2,1,0:T(8,128)(2,1)}) %all-gather.2.cloned.1.call-update) | async-done | bytes 1048592 | tf_op jit(solution)/shard_map/all_gather | solution.py:67
  85.5 0.0 copy-start.1
  85.5 0.0 copy-start.2
  85.5 3.4 %fusion.20 = bf16[128,512]{1,0:T(8,128)(2,1)S(1)} fusion(bf16[1,4096,512]{2,1,0:T(8,128)(2,1)} %param.9, bf16[1,128,4096]{2,1,0:T(8,128)(2,1)} %all-gather.2.cloned.1.call-done), kind=kOutput, calls=%fused_computation.23 | convolution fusion | flops 536936448 | bytes 5373952 | tf_op jit(solution)/shard_map/dot_general | solution.py:70
  88.8 0.4 copy-done.1
  89.2 0.3 copy-done.2
  89.5 0.8 fusion.17
  90.3 0.1 copy.36
  90.5 0.1 copy.37
  90.6 0.0 copy-start.4
  90.6 1.5 fusion.49
  92.1 0.0 copy-start.7
  92.1 0.3 convolution_bitcast_fusion
  92.4 0.7 convolution_convert_fusion.2
  93.1 2.0 convolution_convert_fusion.3
  95.1 0.0 copy-done.4
  95.1 0.0 copy-done.7
  95.2 0.0 copy-start
  95.2 3.8 %fusion.6 = f32[128,4096]{1,0:T(8,128)S(1)} fusion(bf16[128,512]{0,1:T(8,128)(2,1)S(1)} %bitcast.121, bf16[1,4096,512]{2,1,0:T(8,128)(2,1)} %param.8), kind=kOutput, calls=%fused_computation.7 | convolution fusion | flops 536870912 | bytes 6422528 | tf_op jit(solution)/shard_map/skc,dc->skd/dot_general | solution.py:73
  99.0 0.0 copy-done
  99.0 1.5 fusion.2
  100.5 0.0 copy-start.6
  100.5 0.8 convert_element_type.98
  101.3 0.0 copy-start.5
  101.3 0.0 copy-start.8
  101.4 1.3 copy.44
  102.7 0.0 all-reduce.4.cloned.1.call-update
  102.7 0.0 reduce-scatter.10.cloned.1.call-start
  102.8 0.0 copy-done.6
  102.8 0.6 dynamic-slice
  103.4 50.2 %all-reduce.4.cloned.1.call-done = bf16[1,128,4,4,256]{4,1,3,2,0:T(8,128)(2,1)} async-done(((bf16[1,128,4,4,256]{4,1,3,2,0:T(8,128)(2,1)}), bf16[1,128,4,4,256]{4,1,3,2,0:T(8,128)(2,1)}) %all-reduce.4.cloned.1.call-update) | async-done | bytes 1048592
  153.5 2.3 %constant_dynamic-slice_fusion = bf16[1,128,4,1,256]{4,1,3,2,0:T(8,128)(2,1)} fusion(bf16[1,128,4,4,256]{4,1,3,2,0:T(8,128)(2,1)} %all-reduce.4.cloned.1.call-done, u32[]{:T(128)} %bitcast.56), kind=kLoop, calls=%fused_computation.50 | loop fusion | bytes 524292
  155.9 0.0 reduce-scatter.10.cloned.1.call-update
  155.9 1.6 convolution_convert_fusion.1
  157.5 0.0 copy-start.3
  157.5 0.8 copy.45
  158.3 0.0 copy-done.5
  158.3 0.0 copy-done.8
  158.3 2.0 convolution_convert_fusion
  160.3 0.9 copy.46
  161.2 18.8 %reduce-scatter.10.cloned.1.call-done = bf16[1,128,1,1,256]{4,1,3,2,0:T(8,128)(2,1)} async-done(((bf16[1,128,4,1,256]{4,1,3,2,0:T(8,128)(2,1)}), bf16[1,128,1,1,256]{4,1,3,2,0:T(8,128)(2,1)}) %reduce-scatter.10.cloned.1.call-update) | async-done | bytes 65552
  180.0 0.0 copy-done.3
  180.0 1.0 fusion.41
  181.0 41.0 %psum.30 = f32[1,128,1]{1,2,0:T(1,128)S(1)} all-reduce(f32[1,128,1]{1,2,0:T(1,128)S(1)} %bitcast.126), channel_id=1, replica_groups=mesh['section'=4,'dp'=2,'mp'=4] {'section','mp'}, use_global_device_ids=true, to_apply=%region_9.0 | all-reduce | flops 128 | bytes 1024 | tf_op jit(solution)/shard_map/psum | solution.py:87
  222.0 2.5 %psum.31 = f32[256]{0:T(256)S(1)} all-reduce(f32[256]{0:T(256)S(1)} %get-tuple-element.16), channel_id=1, replica_groups=mesh['section'=4,'dp'=2,'mp'=4] {'dp'}, use_global_device_ids=true, to_apply=%region_11.0 | all-reduce | flops 256 | bytes 2048 | tf_op jit(solution)/shard_map/psum | solution.py:88
  224.5 0.6 broadcast_multiply_fusion
  225.0 1.6 fusion.37
  (4 shorter events, 0.1 us)
Async XLA Ops:
  7.2 78.3 %all-gather.2.cloned.1.call-start = ((), (), s32[]{:S(2)}) async-start(), calls=%async_computation.1 | async-start | bytes 1114112 | tf_op jit(solution)/shard_map/all_gather | solution.py:67
  33.9 119.6 %all-reduce.4.cloned.1.call-start = ((), (), s32[]{:S(2)}) async-start(), calls=%async_computation.2 | async-start | bytes 2097152
  85.5 3.7 %copy-start.1 = (bf16[1,4096,512]{2,1,0:T(8,128)(2,1)S(1)}, bf16[1,4096,512]{2,1,0:T(8,128)(2,1)}, u32[]{:S(2)}) copy-start(bf16[1,4096,512]{2,1,0:T(8,128)(2,1)} %param.8) | copy-start | bytes 12582916
  85.5 4.0 %copy-start.2 = (bf16[1,128,4096]{2,1,0:T(8,128)(2,1)S(1)}, bf16[1,128,4096]{2,1,0:T(8,128)(2,1)}, u32[]{:S(2)}) copy-start(bf16[1,128,4096]{2,1,0:T(8,128)(2,1)} %all-gather.2.cloned.1.call-done) | copy-start | bytes 3145732
  90.6 4.5 %copy-start.4 = (bf16[1,128,512]{1,2,0:T(8,128)(2,1)}, bf16[1,128,512]{1,2,0:T(8,128)(2,1)S(1)}, u32[]{:S(2)}) copy-start(bf16[1,128,512]{1,2,0:T(8,128)(2,1)S(1)} %copy.37) | copy-start | bytes 393220
  92.1 3.1 %copy-start.7 = (f32[8,256]{1,0:T(8,128)}, f32[8,256]{1,0:T(8,128)S(1)}, u32[]{:S(2)}) copy-start(f32[8,256]{1,0:T(8,128)S(1)} %get-tuple-element.20) | copy-start | bytes 24580
  95.2 3.8 %copy-start = (bf16[1,4096,512]{2,1,0:T(8,128)(2,1)S(1)}, bf16[1,4096,512]{2,1,0:T(8,128)(2,1)}, u32[]{:S(2)}) copy-start(bf16[1,4096,512]{2,1,0:T(8,128)(2,1)} %param.9) | copy-start | bytes 12582916
  100.5 2.2 copy-start.6
  101.3 57.0 %copy-start.5 = (bf16[1,128,512]{1,2,0:T(8,128)(2,1)S(1)}, bf16[1,128,512]{1,2,0:T(8,128)(2,1)}, u32[]{:S(2)}) copy-start(bf16[1,128,512]{1,2,0:T(8,128)(2,1)} %copy-done.4) | copy-start | bytes 393220
  101.3 57.0 %copy-start.8 = (f32[8,256]{1,0:T(8,128)S(1)}, f32[8,256]{1,0:T(8,128)}, u32[]{:S(2)}) copy-start(f32[8,256]{1,0:T(8,128)} %copy-done.7) | copy-start | bytes 24580
  102.7 77.3 %reduce-scatter.10.cloned.1.call-start = ((), (), s32[]{:S(2)}) async-start(), calls=%async_computation.3 | async-start | bytes 327680
  157.5 22.5 %copy-start.3 = (bf16[1,128,256]{2,1,0:T(8,128)(2,1)S(1)}, bf16[1,128,256]{2,1,0:T(8,128)(2,1)}, u32[]{:S(2)}) copy-start(bf16[1,128,256]{2,1,0:T(8,128)(2,1)} %param.6) | copy-start | bytes 196612
Sparse Core Ops, SparseCore 0:
  34.0 51.4 all-gather.1
  102.8 50.6 all-reduce.3
  156.5 23.4 reduce-scatter.9
